TPU v7x, 32 devices: a whole 2x2x4 slice. The times are simulated.
32 devices in a mesh: group: 2 (over y), tile: 8 (over z, x), lev: 2 (over core).
Axes of the slice: x: 2, y: 2, z: 4, core: 2. Of those that a mesh axis runs over, the one named last changes fastest.
Arguments:
- members_x: bfloat16 [80, 32, 32768], P(None, 'lev', ('group', 'tile')), parts along dimension 2, may hold values from -6 to 6
- error_early: bfloat16 [32, 32768], P('lev', ('group', 'tile')), parts along dimension 1, may hold values from -6 to 6
- error_late: bfloat16 [32, 32768], P('lev', ('group', 'tile')), parts along dimension 1, may hold values from -6 to 6
- energy: bfloat16 [32, 32768], P('lev', ('group', 'tile')), parts along dimension 1, may hold values from 0.29882812 to 3
- vert_weight: float32 [8, 32], replicated, may hold values from 0.05 to 1
- tile_lists: int32 [16, 2, 3], P(('group', 'tile')), parts along dimension 0, may hold values from 0 to 7, as said below
- obs_block: int32 [16, 4096], P(('group', 'tile')), parts along dimension 0, may hold values from 0 to 1, never falling along the last dimension, each value on 1 to 4095 neighbouring positions
- obs_bin: int32 [16, 4096], P(('group', 'tile')), parts along dimension 0, may hold values from 0 to 7
- obs_column: int32 [16, 4096], P(('group', 'tile')), parts along dimension 0, may hold values from 0 to 2047
- obs_pert: bfloat16 [16, 80, 4096], P(('group', 'tile')), parts along dimension 0, may hold values from -6 to 6
- innovation: float32 [16, 4096], P(('group', 'tile')), parts along dimension 0, may hold values from -6 to 6
- inv_variance: float32 [16, 4096], P(('group', 'tile')), parts along dimension 0, may hold values from 0.25 to 4
- horiz_weight: float32 [16, 4, 4096], P(('group', 'tile')), parts along dimension 0, may hold values from 0.1 to 1
Outputs:
- impact: float32 [16, 2048, 2], P(('group', 'tile'), None, 'lev'), parts along dimension 0
There are 2 independent parts, one for each index of `group`. A program takes and returns all parts, laid end to end along the dimension named above; an argument that names none is the same for every part. Nothing has to cross between parts.
Inputs may be any that keep to these rules, and one draw needn't show every extreme that they name: `tile_lists`: in each row, the 2 * (3) entries are distinct tiles and none is the row's own tile. `obs_block`: within a row block numbers never fall; every block of a row holds 1 to 4095 observations.
All inputs are finite; a program needn't handle non-finite values.
Results may differ from a plain program's by a relative error of at most 0.0029.
Values may be sent and summed in bfloat16 or wider, within the bound.
A program may use at most 64 MiB of HBM per device.

v0:
```python
import jax
import jax.numpy as jnp
from jax import lax
from jax.sharding import PartitionSpec as P


def pick_level(values, lev_place, lev_count):
    shaped = values.reshape(values.shape[:-1] + (values.shape[-1] // lev_count, lev_count))
    return lax.dynamic_slice_in_dim(shaped, lev_place, 1, shaped.ndim - 1)[..., 0]


def on_device(
    members_x,
    error_early,
    error_late,
    energy,
    vert_weight,
    tile_lists,
    obs_block,
    obs_bin,
    obs_column,
    obs_pert,
    innovation,
    inv_variance,
    horiz_weight,
):
    lev_count = lax.axis_size("lev")
    lev_place = lax.axis_index("lev")
    peers = lax.axis_size("tile")
    members = members_x.shape[0]
    levels_here = members_x.shape[1]
    columns = members_x.shape[2]
    bins_all = vert_weight.shape[0]
    tile_table = tile_lists[0]
    blocks = tile_table.shape[0]
    later_slots = tile_table.shape[1]
    obs_count = obs_block.shape[1]
    largest = min(2 * obs_count // blocks, obs_count - blocks + 1)
    capacity = (largest + lev_count - 1) // lev_count
    share_obs = obs_count // lev_count
    lane_width = (members + 127) // 128 * 128
    scaled = energy.astype(jnp.float32) * (
        error_early.astype(jnp.float32) + error_late.astype(jnp.float32)
    )
    local_vert = lax.dynamic_slice_in_dim(vert_weight, lev_place * levels_here, levels_here, 1)
    weighted = members_x.astype(jnp.float32) * scaled[None]
    partial_value = jnp.einsum("bl,klc->bck", local_vert, weighted, precision=lax.Precision.HIGHEST)
    summary = lax.psum(partial_value, "lev").astype(jnp.bfloat16)
    summary_rows = jnp.pad(
        summary.reshape(bins_all * columns, members), ((0, 0), (0, lane_width - members))
    )
    lookup_mine = pick_level(obs_bin[0] * columns + obs_column[0], lev_place, lev_count)
    pert_rows = pick_level(obs_pert[0], lev_place, lev_count).T.astype(jnp.float32)
    pert_rows = jnp.pad(pert_rows, ((0, 0), (0, lane_width - members)))
    weight_mine = pick_level(horiz_weight[0], lev_place, lev_count)
    block_mine = pick_level(obs_block[0], lev_place, lev_count)
    own_values = jnp.take(summary_rows, lookup_mine, axis=0)
    own_dots = jnp.sum(own_values.astype(jnp.float32) * pert_rows, axis=1)
    total = weight_mine[0] * own_dots
    block_ids = jnp.arange(blocks, dtype=jnp.int32)
    in_block = (obs_block[0][None, :] == block_ids[:, None]).astype(jnp.int32)
    sizes = jnp.sum(in_block, axis=1)
    starts = jnp.cumsum(sizes) - sizes
    firsts = starts + (lev_place - starts) % lev_count
    base_local = (firsts - lev_place) // lev_count
    entries = tile_table.reshape(-1)
    entry_ids = jnp.arange(entries.shape[0], dtype=jnp.int32)
    match = (entries[None, :] == jnp.arange(peers, dtype=jnp.int32)[:, None]).astype(jnp.int32)
    listed = jnp.sum(match, axis=1) > 0
    peer_block = jnp.sum(match * (entry_ids // later_slots)[None, :], axis=1)
    slot_ids = jnp.arange(capacity, dtype=jnp.int32)
    obs_index = firsts[peer_block][:, None] + lev_count * slot_ids[None, :]
    ends = (starts + sizes)[peer_block][:, None]
    valid = listed[:, None] & (obs_index < ends)
    local_index = jnp.where(valid, (obs_index - lev_place) // lev_count, 0).reshape(-1)
    valid = valid.reshape(-1)
    outgoing = jnp.where(valid, lookup_mine[local_index], -1)
    wanted = lax.all_to_all(outgoing, "tile", split_axis=0, concat_axis=0, tiled=True)
    present = wanted >= 0
    fetched = jnp.take(summary_rows, jnp.maximum(wanted, 0), axis=0)
    fetched = jnp.where(present[:, None], fetched, jnp.zeros_like(fetched))
    replies = lax.all_to_all(fetched, "tile", split_axis=0, concat_axis=0, tiled=True)
    block_onehot = (block_mine[:, None] == block_ids[None, :]).astype(jnp.int32)
    slot_mine = jnp.arange(share_obs, dtype=jnp.int32) - jnp.sum(
        block_onehot * base_local[None, :], axis=1
    )
    for entry in range(1, later_slots + 1):
        peer_mine = jnp.sum(block_onehot * tile_table[:, entry - 1][None, :], axis=1)
        row_mine = peer_mine * capacity + slot_mine
        remote_values = jnp.take(replies, row_mine, axis=0)
        remote_dots = jnp.sum(remote_values.astype(jnp.float32) * pert_rows, axis=1)
        total = total + weight_mine[entry] * remote_dots
    obs_scale = (
        pick_level(innovation[0], lev_place, lev_count)
        * pick_level(inv_variance[0], lev_place, lev_count)
        / (members - 1.0)
    )
    impact = obs_scale * total
    return impact[None, :, None]


def solution(mesh):
    return jax.shard_map(
        on_device,
        mesh=mesh,
        in_specs=(
            P(None, "lev", ("group", "tile")),
            P("lev", ("group", "tile")),
            P("lev", ("group", "tile")),
            P("lev", ("group", "tile")),
            P(),
            P(("group", "tile"), None, None),
            P(("group", "tile"), None),
            P(("group", "tile"), None),
            P(("group", "tile"), None),
            P(("group", "tile"), None, None),
            P(("group", "tile"), None),
            P(("group", "tile"), None),
            P(("group", "tile"), None, None),
        ),
        out_specs=P(("group", "tile"), None, "lev"),
        check_vma=False,
    )
```

profile of v0, /device:TPU:0, one launch (start us, length us, event | category | flops | bytes accessed | tf_op | source)
XLA Modules:
  0.0 342.2 jit_solution(14664522143989487243)
XLA Ops:
  0.0 0.0 copy-start
  0.0 0.9 fusion.16
  0.9 0.2 reduce-window.7
  1.1 0.8 eq.47
  1.9 0.1 convert_reduce_fusion
  2.0 0.6 gather_fusion
  2.7 0.6 gather_fusion.1
  3.3 0.1 fusion.11
  3.4 0.1 fusion.15
  3.5 0.1 copy.52
  3.6 0.1 copy.53
  3.6 0.4 compare_select_fusion
  4.1 0.5 broadcast.472
  4.6 1.4 reduce.31
  6.0 1.0 reshape_squeeze.19
  7.0 0.8 add_reduce_fusion
  7.8 1.0 add.161
  8.8 1.2 dynamic-slice_reduce_fusion
  10.0 0.0 copy-start.3
  10.0 0.0 copy-start.4
  10.0 0.0 copy-start.5
  10.0 90.5 %gather_fusion.2 = s32[16384]{0:T(1024)S(1)} fusion(s32[2048]{0:T(1024)S(1)} %get-tuple-element.34, s32[16384]{0:T(1024)S(1)} %broadcast_clamp_fusion.1), kind=kCustom, calls=%fused_computation.6 | custom fusion | bytes 196608 | tf_op jit(solution)/shard_map/gather | solution.py:77
  100.6 0.1 fusion.13
  100.7 0.7 copy.43
  101.4 7.3 %all-to-all-start = ((s32[8,2048,1]{1,2,0:T(1,128)}), s32[8,2048,1]{1,2,0:T(1,128)S(1)}, u32[]{:S(2)}, u32[]{:S(2)}) async-start(s32[8,2048,1]{1,2,0:T(1,128)} %copy.43), calls=%async_computation | async-start | bytes 131072 | tf_op jit(solution)/shard_map/all_to_all | solution.py:78
  108.6 0.0 copy-done.3
  108.6 0.0 copy-done.4
  108.6 0.0 copy-done.5
  108.7 10.9 %fusion.4 = f32[8,2048,80]{1,0,2:T(8,128)} fusion(bf16[80,16,2048]{2,1,0:T(8,128)(2,1)} %param.15, f32[16,2048]{1,0:T(8,128)S(1)} %add_multiply_fusion, f32[8,32]{1,0:T(8,128)S(1)} %copy-done, s32[]{:T(128)S(6)} %select_n.116), kind=kOutput, calls=%fused_computation.13 | convolution fusion | flops 256901120 | bytes 10617860 | tf_op jit(solution)/shard_map/bl,klc->bck/dot_general | solution.py:47
  119.6 17.6 %all-reduce.4 = bf16[8,2048,80]{1,0,2:T(8,128)(2,1)S(1)} all-reduce(f32[8,2048,80]{1,0,2:T(8,128)} %fusion.4), channel_id=1, replica_groups=mesh['group'=2,'tile'=8,'lev'=2] {'lev'}, use_global_device_ids=true, to_apply=%region_0.0 | all-reduce | flops 1310720 | bytes 7864320 | tf_op jit(solution)/shard_map/psum | solution.py:48
  137.2 4.3 %copy.46 = bf16[8,2048,80]{2,1,0:T(8,128)(2,1)} copy(bf16[8,2048,80]{1,0,2:T(8,128)(2,1)S(1)} %all-reduce.4) | data formatting | bytes 5242880 | tf_op jit(solution)/shard_map/reshape | solution.py:50
  141.5 0.0 all-to-all-done
  141.5 0.1 broadcast_maximum_fusion
  141.6 0.4 compare_reduce_fusion.1
  142.1 57.8 %gather_fusion.3 = bf16[16384,80]{1,0:T(8,128)(2,1)} fusion(bf16[16384,80]{1,0:T(8,128)(2,1)} %bitcast.48, s32[16384]{0:T(1024)S(1)} %broadcast_clamp_fusion), kind=kCustom, calls=%fused_computation.7 | custom fusion | bytes 5308416 | tf_op jit(solution)/shard_map/jit(_take)/gather | solution.py:80
  199.9 13.8 %select_select_fusion = bf16[16384,128]{1,0:T(8,128)(2,1)} fusion(bf16[16384,80]{1,0:T(8,128)(2,1)} %gather_fusion.3, pred[16384]{0:T(1024)(128)(4,1)S(1)} %bitcast.59, pred[16384]{0:T(1024)(128)(4,1)S(1)} %bitcast.58), kind=kLoop, calls=%fused_computation.12 | loop fusion | flops 4194304 | bytes 6848512 | tf_op jit(solution)/shard_map/jit(_where)/select_n | solution.py:81
  213.6 6.0 %all-to-all-start.1 = ((bf16[8,2048,128]{2,1,0:T(8,128)(2,1)}), bf16[8,2048,128]{2,1,0:T(8,128)(2,1)}, u32[]{:S(2)}, u32[]{:S(2)}) async-start(bf16[8,2048,128]{2,1,0:T(8,128)(2,1)} %bitcast.51), calls=%async_computation.1 | async-start | bytes 8388608 | tf_op jit(solution)/shard_map/all_to_all | solution.py:82
  219.6 4.0 %pad.12 = bf16[16384,128]{1,0:T(8,128)(2,1)} pad(bf16[16384,80]{1,0:T(8,128)(2,1)} %bitcast.49, bf16[]{:T(256)} %constant.99.clone.1), padding=0_0x0_48 | pad | bytes 6815746 | tf_op jit(solution)/shard_map/jit(_pad)/pad | solution.py:49
  223.7 0.6 copy.40
  224.3 1.1 constant_dynamic-slice_fusion.2
  225.5 0.9 copy.57
  226.3 0.6 copy.37
  227.0 8.5 %constant_dynamic-slice_fusion.1 = (f32[1,2048,1]{0,2,1:T(1,128)}, f32[1,2048,1]{0,2,1:T(1,128)}, f32[1,2048,1]{0,2,1:T(1,128)}, f32[1,2048,1]{0,2,1:T(1,128)S(1)}) fusion(f32[4,2048,2]{0,2,1:T(2,128)S(1)} %bitcast.50, s32[]{:T(128)S(6)} %select_n.115, s32[]{:T(128)S(6)} %add.210, s32[]{:T(128)S(6)} %add.209, s32[]{:T(128)S(6)} %add.211), kind=kLoop, calls=%fused_computation.76 | loop fusion | bytes 65552 | tf_op jit(solution)/shard_map/slice | solution.py:59
  235.5 2.3 copy.48
  237.7 2.3 copy.49
  240.0 2.3 copy.50
  242.3 0.6 copy.51
  242.9 0.5 broadcast.470
  243.4 0.0 copy-done.7
  243.4 0.7 reduce.30
  244.1 1.0 reshape_squeeze.15
  245.1 0.0 copy-start.9
  245.1 0.7 reduce.29
  245.8 1.0 reshape_squeeze.16
  246.8 8.3 %gather_fusion.4 = bf16[2048,128]{1,0:T(8,128)(2,1)S(1)} fusion(bf16[16384,128]{1,0:T(8,128)(2,1)} %pad.12, s32[2048]{0:T(1024)S(1)} %fusion.17), kind=kCustom, calls=%fused_computation.clone | custom fusion | bytes 1056768 | tf_op jit(solution)/shard_map/jit(_take)/gather | solution.py:57
  255.2 0.9 multiply_reduce_fusion
  256.1 0.2 slice_reduce_fusion.2
  256.3 0.1 select_reduce_fusion.3
  256.5 56.9 %all-to-all-done.1 = bf16[8,2048,128]{2,1,0:T(8,128)(2,1)} async-done(((bf16[8,2048,128]{2,1,0:T(8,128)(2,1)}), bf16[8,2048,128]{2,1,0:T(8,128)(2,1)}, u32[]{:S(2)}, u32[]{:S(2)}) %all-to-all-start.1) | async-done | bytes 4194336 | tf_op jit(solution)/shard_map/all_to_all | solution.py:82
  313.4 8.3 %gather_fusion.6 = bf16[2048,128]{1,0:T(8,128)(2,1)S(1)} fusion(bf16[16384,128]{1,0:T(8,128)(2,1)} %bitcast.17, s32[2048]{0:T(1024)S(1)} %get-tuple-element.31), kind=kCustom, calls=%fused_computation.2.clone | custom fusion | bytes 1056768 | tf_op jit(solution)/shard_map/jit(_take)/gather | solution.py:90
  321.8 8.4 %gather_fusion.7 = bf16[2048,128]{1,0:T(8,128)(2,1)S(1)} fusion(bf16[16384,128]{1,0:T(8,128)(2,1)} %bitcast.17, s32[2048]{0:T(1024)S(1)} %get-tuple-element.32), kind=kCustom, calls=%fused_computation.3.clone | custom fusion | bytes 1056768 | tf_op jit(solution)/shard_map/jit(_take)/gather | solution.py:90
  330.2 8.3 %gather_fusion.5 = bf16[2048,128]{1,0:T(8,128)(2,1)S(1)} fusion(bf16[16384,128]{1,0:T(8,128)(2,1)} %bitcast.17, s32[2048]{0:T(1024)S(1)} %get-tuple-element.30), kind=kCustom, calls=%fused_computation.1.clone | custom fusion | bytes 1056768 | tf_op jit(solution)/shard_map/jit(_take)/gather | solution.py:90
  338.6 3.0 fusion.7
  341.6 0.6 add_multiply_fusion.1
  (27 shorter events, 0.2 us)
Async XLA Ops:
  0.0 108.7 %copy-start = (f32[8,32]{1,0:T(8,128)S(1)}, f32[8,32]{1,0:T(8,128)}, u32[]{:S(2)}) copy-start(f32[8,32]{1,0:T(8,128)} %param.19) | copy-start | bytes 3076
  10.0 98.6 %copy-start.3 = (bf16[16,2048]{1,0:T(8,128)(2,1)S(1)}, bf16[16,2048]{1,0:T(8,128)(2,1)}, u32[]{:S(2)}) copy-start(bf16[16,2048]{1,0:T(8,128)(2,1)} %param.17) | copy-start | bytes 196612
  10.0 98.6 %copy-start.4 = (bf16[16,2048]{1,0:T(8,128)(2,1)S(1)}, bf16[16,2048]{1,0:T(8,128)(2,1)}, u32[]{:S(2)}) copy-start(bf16[16,2048]{1,0:T(8,128)(2,1)} %param.16) | copy-start | bytes 196612
  10.0 98.6 %copy-start.5 = (bf16[16,2048]{1,0:T(8,128)(2,1)S(1)}, bf16[16,2048]{1,0:T(8,128)(2,1)}, u32[]{:S(2)}) copy-start(bf16[16,2048]{1,0:T(8,128)(2,1)} %param.18) | copy-start | bytes 196612
  101.4 40.1 %all-to-all-start = ((s32[8,2048,1]{1,2,0:T(1,128)}), s32[8,2048,1]{1,2,0:T(1,128)S(1)}, u32[]{:S(2)}, u32[]{:S(2)}) async-start(s32[8,2048,1]{1,2,0:T(1,128)} %copy.43), calls=%async_computation | async-start | bytes 131072 | tf_op jit(solution)/shard_map/all_to_all | solution.py:78
  213.6 99.8 %all-to-all-start.1 = ((bf16[8,2048,128]{2,1,0:T(8,128)(2,1)}), bf16[8,2048,128]{2,1,0:T(8,128)(2,1)}, u32[]{:S(2)}, u32[]{:S(2)}) async-start(bf16[8,2048,128]{2,1,0:T(8,128)(2,1)} %bitcast.51), calls=%async_computation.1 | async-start | bytes 8388608 | tf_op jit(solution)/shard_map/all_to_all | solution.py:82
  219.6 4.1 %copy-start.2 = (bf16[1,80,4096]{2,1,0:T(8,128)(2,1)S(1)}, bf16[1,80,4096]{2,1,0:T(8,128)(2,1)}, u32[]{:S(2)}) copy-start(bf16[1,80,4096]{2,1,0:T(8,128)(2,1)} %param.24) | copy-start | bytes 1966084
  223.7 2.7 copy-start.6
  235.5 7.9 %copy-start.7 = (f32[1,4096]{1,0:T(1,128)S(1)}, f32[1,4096]{1,0:T(1,128)}, u32[]{:S(2)}) copy-start(f32[1,4096]{1,0:T(1,128)} %param.25) | copy-start | bytes 49156
  235.5 9.6 %copy-start.8 = (f32[1,4096]{1,0:T(1,128)S(1)}, f32[1,4096]{1,0:T(1,128)}, u32[]{:S(2)}) copy-start(f32[1,4096]{1,0:T(1,128)} %param.26) | copy-start | bytes 49156
  245.1 11.0 %copy-start.9 = (s32[1,2,3]{2,1,0:T(2,128)S(1)}, s32[1,2,3]{2,1,0:T(2,128)}, u32[]{:S(2)}) copy-start(s32[1,2,3]{2,1,0:T(2,128)} %param.20) | copy-start | bytes 76
  321.8 16.8 %copy-start.1 = (bf16[80,2048,1]{0,1,2:T(8,128)(2,1)S(1)}, bf16[80,2048,1]{0,1,2:T(8,128)(2,1)}, u32[]{:S(2)}) copy-start(bf16[80,2048,1]{0,1,2:T(8,128)(2,1)} %copy.57) | copy-start | bytes 983044
where the time goes:
time: 343 us; the launch traced here: 342 us
  local copies, waits for them, and re-layouts  219 us (64%)
  waiting for transfers between devices  56.9 us (17%)
  other arithmetic  24.5 us (7%)
  blocking collectives  17.6 us (5%)
  starting transfers between devices  13.2 us (4%)
  matrix products  10.9 us (3%)
    gather x2, local copies, waits for them, and re-layouts, on_device(): outgoing = jnp.where(valid, lookup_mine[local_index], -1)  90.6 us
    gather x1, local copies, waits for them, and re-layouts, on_device(): fetched = jnp.take(summary_rows, jnp.maximum(wanted, 0), axis=0)  57.8 us
    all_to_all x1, waiting for transfers between devices, on_device(): lax.all_to_all(fetched, 'tile', split_axis=0, concat_axis=0, tiled=True)  56.9 us
    gather x3, local copies, waits for them, and re-layouts, on_device(): remote_values = jnp.take(replies, row_mine, axis=0)  25.1 us
    psum x1, blocking collectives, on_device(): summary = lax.psum(partial_value, 'lev').astype(jnp.bfloat16)  17.6 us
    select_n x1, other arithmetic, on_device(): fetched = jnp.where(present[:, None], fetched, jnp.zeros_like(fetched))  13.8 us
    dot_general x1, matrix products, on_device(): jnp.einsum('bl,klc->bck', local_vert, weighted, precision=lax.Precision.H...  10.9 us
    unnamed x32, local copies, waits for them, and re-layouts  9.93 us
  transfers between devices with their start and end apart: 2, of which 1 were waited for; matrix products, arithmetic and copies ran while one was open for 15% of the time, Pallas kernels for 0%

commit v1 on v0

v1 whole, which is shorter than its diff:
```python
import functools

import jax
import jax.numpy as jnp
from jax import lax
from jax.experimental import pallas as pl
from jax.experimental.pallas import tpu as pltpu
from jax.sharding import PartitionSpec as P

CHUNK = 256
LANES = 128
VMEM_LIMIT = 56 * 1024 * 1024


def pick_level(values, lev_place, lev_count):
    shaped = values.reshape(values.shape[:-1] + (values.shape[-1] // lev_count, lev_count))
    return lax.dynamic_slice_in_dim(shaped, lev_place, 1, shaped.ndim - 1)[..., 0]


def split_high_low(values):
    high = values.astype(jnp.bfloat16)
    low = (values - high.astype(jnp.float32)).astype(jnp.bfloat16)
    return high, low


def partial_kernel(group, members_ref, early_ref, late_ref, energy_ref, weight_ref, own_ref, sent_ref):
    members, levels, width = members_ref.shape
    bins = own_ref.shape[0]
    scaled = energy_ref[...].astype(jnp.float32) * (
        early_ref[...].astype(jnp.float32) + late_ref[...].astype(jnp.float32)
    )
    rows = bins * group
    weight = weight_ref[...]
    for part in range(members // group):
        block = members_ref[part * group:(part + 1) * group].astype(jnp.float32) * scaled[None]
        high, low = split_high_low(block.reshape(group * levels, width))
        both = jnp.dot(weight, high, preferred_element_type=jnp.float32)
        summed = both[:rows] + both[rows:]
        summed = summed + jnp.dot(weight[:rows], low, preferred_element_type=jnp.float32)
        shaped = summed.reshape(bins, group, width)
        own_ref[:, part * group:(part + 1) * group, :] = shaped
        sent_ref[:, part * group:(part + 1) * group, :] = shaped.astype(jnp.bfloat16)


def partial_summary(members_x, error_early, error_late, energy, local_vert):
    members, levels, columns = members_x.shape
    bins = local_vert.shape[0]
    group = 16
    width = min(512, columns)
    eye = jnp.eye(group, dtype=jnp.float32)
    weight = (local_vert[:, None, None, :] * eye[None, :, :, None]).reshape(bins * group, group * levels)
    weight = jnp.concatenate(split_high_low(weight), axis=0)
    field = pl.BlockSpec((levels, width), lambda i: (0, i))
    out = pl.BlockSpec((bins, members, width), lambda i: (0, 0, i))
    return pl.pallas_call(
        functools.partial(partial_kernel, group),
        grid=(columns // width,),
        in_specs=[
            pl.BlockSpec((members, levels, width), lambda i: (0, 0, i)),
            field,
            field,
            field,
            pl.BlockSpec(weight.shape, lambda i: (0, 0)),
        ],
        out_specs=[out, out],
        out_shape=[
            jax.ShapeDtypeStruct((bins, members, columns), jnp.float32),
            jax.ShapeDtypeStruct((bins, members, columns), jnp.bfloat16),
        ],
        compiler_params=pltpu.CompilerParams(vmem_limit_bytes=VMEM_LIMIT),
        name="partial_summary",
    )(members_x, error_early, error_late, energy, weight)


def dots_kernel(bins, first_ref, last_ref, own_ref, other_ref, lookup_ref, pert_ref, dots_ref, table_ref, rows_ref):
    step = pl.program_id(0)
    members, columns = own_ref.shape[1], own_ref.shape[2]

    @pl.when(step < bins)
    def _():
        for start in range(0, columns, LANES):
            here = slice(start, start + LANES)
            summed = own_ref[0, :, here] + other_ref[0, :, here].astype(jnp.float32)
            padded = jnp.concatenate(
                [summed, jnp.zeros((LANES - members, LANES), jnp.float32)], axis=0
            )
            place = pl.multiple_of(step * columns + start, LANES)
            table_ref[pl.ds(place, LANES), :] = padded.T

    @pl.when(step >= bins)
    def _():
        owner = step - bins
        dots_ref[...] = jnp.zeros_like(dots_ref)
        row_id = lax.broadcasted_iota(jnp.int32, (LANES, LANES), 0)
        col_id = lax.broadcasted_iota(jnp.int32, (LANES, LANES), 1)

        def one_chunk(chunk, carry):
            base = pl.multiple_of(chunk * CHUNK, CHUNK)
            for place in range(CHUNK):
                index = lookup_ref[0, 0, base + place]
                rows_ref[pl.ds(place, 1), :] = table_ref[pl.ds(index, 1), :]
            for sub in range(0, CHUNK, LANES):
                values = rows_ref[sub:sub + LANES, :members]
                high, low = split_high_low(values)
                here = pl.ds(pl.multiple_of(base + sub, LANES), LANES)
                pert = pert_ref[0, :, here]
                product = jnp.dot(high, pert, preferred_element_type=jnp.float32) + jnp.dot(
                    low, pert, preferred_element_type=jnp.float32
                )
                picked = jnp.where(row_id == col_id, product, 0.0)
                dots_ref[0, :, here] = jnp.sum(picked, axis=0, keepdims=True)
            return carry

        lax.fori_loop(first_ref[owner], last_ref[owner], one_chunk, 0)


def tile_dots(own, other, lookups, perts, first, last):
    bins, members, columns = own.shape
    peers, _, share = lookups.shape
    return pl.pallas_call(
        functools.partial(dots_kernel, bins),
        grid_spec=pltpu.PrefetchScalarGridSpec(
            num_scalar_prefetch=2,
            grid=(bins + peers,),
            in_specs=[
                pl.BlockSpec((1, members, columns), lambda i, *_: (jnp.minimum(i, bins - 1), 0, 0)),
                pl.BlockSpec((1, members, columns), lambda i, *_: (jnp.minimum(i, bins - 1), 0, 0)),
                pl.BlockSpec(
                    (1, 1, share), lambda i, *_: (jnp.maximum(i - bins, 0), 0, 0), memory_space=pltpu.SMEM
                ),
                pl.BlockSpec((1, members, share), lambda i, *_: (jnp.maximum(i - bins, 0), 0, 0)),
            ],
            out_specs=pl.BlockSpec((1, 1, share), lambda i, *_: (jnp.maximum(i - bins, 0), 0, 0)),
            scratch_shapes=[
                pltpu.VMEM((bins * columns, LANES), jnp.float32),
                pltpu.VMEM((CHUNK, LANES), jnp.float32),
            ],
        ),
        out_shape=jax.ShapeDtypeStruct((peers, 1, share), jnp.float32),
        compiler_params=pltpu.CompilerParams(vmem_limit_bytes=VMEM_LIMIT),
        name="tile_dots",
    )(first, last, own, other, lookups, perts)


def on_device(
    members_x,
    error_early,
    error_late,
    energy,
    vert_weight,
    tile_lists,
    obs_block,
    obs_bin,
    obs_column,
    obs_pert,
    innovation,
    inv_variance,
    horiz_weight,
):
    lev_count = lax.axis_size("lev")
    lev_place = lax.axis_index("lev")
    peers = lax.axis_size("tile")
    tile_place = lax.axis_index("tile")
    members = members_x.shape[0]
    levels_here = members_x.shape[1]
    columns = members_x.shape[2]
    tile_table = tile_lists[0]
    blocks = tile_table.shape[0]
    later_slots = tile_table.shape[1]
    obs_count = obs_block.shape[1]
    share = obs_count // lev_count

    half = lev_place * share
    perts = lax.all_gather(lax.dynamic_slice_in_dim(obs_pert[0], half, share, 1), "tile")
    lookup_half = lax.dynamic_slice_in_dim(obs_bin[0] * columns + obs_column[0], half, share, 0)

    tile_ids = jnp.arange(peers, dtype=jnp.int32)
    block_ids = jnp.arange(blocks, dtype=jnp.int32)
    starts = jnp.sum((obs_block[0][None, :] < block_ids[:, None]).astype(jnp.int32), axis=1)
    ends = jnp.sum((obs_block[0][None, :] <= block_ids[:, None]).astype(jnp.int32), axis=1)
    listed = jnp.any(tile_table[:, :, None] == tile_ids[None, None, :], axis=1)
    range_first = jnp.sum(jnp.where(listed, starts[:, None], 0), axis=0)
    range_last = jnp.sum(jnp.where(listed, ends[:, None], 0), axis=0)
    range_first = jnp.where(tile_ids == tile_place, 0, range_first)
    range_last = jnp.where(tile_ids == tile_place, obs_count, range_last)
    range_first = jnp.clip(range_first - half, 0, share)
    range_last = jnp.clip(range_last - half, 0, share)
    packed = jnp.concatenate([lookup_half, range_first, range_last])
    everyone = lax.all_gather(packed, "tile")
    lookups = everyone[:, :share].reshape(peers, 1, share)
    first = lax.dynamic_slice_in_dim(everyone, share + tile_place, 1, 1)[:, 0]
    last = lax.dynamic_slice_in_dim(everyone, share + peers + tile_place, 1, 1)[:, 0]
    first_chunk = first // CHUNK
    last_chunk = jnp.where(last > first, (last + CHUNK - 1) // CHUNK, first_chunk)

    local_vert = lax.dynamic_slice_in_dim(vert_weight, lev_place * levels_here, levels_here, 1)
    own, sent = partial_summary(members_x, error_early, error_late, energy, local_vert)
    other = lax.ppermute(sent, "lev", [(i, (i + 1) % lev_count) for i in range(lev_count)])
    dots = tile_dots(own, other, lookups, perts, first_chunk, last_chunk)

    by_parity = jnp.moveaxis(dots.reshape(peers, share // lev_count, lev_count), 2, 1)
    by_parity = by_parity.reshape(peers * lev_count, share // lev_count)
    returned = lax.all_to_all(by_parity, ("tile", "lev"), split_axis=0, concat_axis=0, tiled=True)
    returned = returned.reshape(peers, share)

    block_mine = pick_level(obs_block[0], lev_place, lev_count)
    weight_mine = pick_level(horiz_weight[0], lev_place, lev_count)
    block_onehot = (block_mine[:, None] == block_ids[None, :]).astype(jnp.int32)
    total = jnp.where(tile_ids[:, None] == tile_place, weight_mine[0][None, :], 0.0)
    for entry in range(1, later_slots + 1):
        peer_mine = jnp.sum(block_onehot * tile_table[:, entry - 1][None, :], axis=1)
        total = total + jnp.where(
            tile_ids[:, None] == peer_mine[None, :], weight_mine[entry][None, :], 0.0
        )
    obs_scale = (
        pick_level(innovation[0], lev_place, lev_count)
        * pick_level(inv_variance[0], lev_place, lev_count)
        / (members - 1.0)
    )
    impact = obs_scale * jnp.sum(total * returned, axis=0)
    return impact[None, :, None]


def solution(mesh):
    return jax.shard_map(
        on_device,
        mesh=mesh,
        in_specs=(
            P(None, "lev", ("group", "tile")),
            P("lev", ("group", "tile")),
            P("lev", ("group", "tile")),
            P("lev", ("group", "tile")),
            P(),
            P(("group", "tile"), None, None),
            P(("group", "tile"), None),
            P(("group", "tile"), None),
            P(("group", "tile"), None),
            P(("group", "tile"), None, None),
            P(("group", "tile"), None),
            P(("group", "tile"), None),
            P(("group", "tile"), None, None),
        ),
        out_specs=P(("group", "tile"), None, "lev"),
        check_vma=False,
    )
```

time: 343 us -> 192 us (0.56)
  local copies, waits for them, and re-layouts: 219 us -> 60.7 us
  Pallas kernels: 0 us -> 36.5 us
  blocking collectives: 17.6 us -> 0 us
  other arithmetic: 24.5 us -> 9.43 us
  between operations: 0.41 us -> 14.2 us
  matrix products: 10.9 us -> 0 us
  starting transfers between devices: 13.2 us -> 4.05 us
  waiting for transfers between devices: 56.9 us -> 65 us
    gather x9 -> x0, local copies, waits for them, and re-layouts: 183 us -> none  [the longest x2 90.6 us: on_device(): outgoing = jnp.where(valid, lookup_mine[local_index], -1)]
    all_gather x0 -> x1, waiting for transfers between devices: none -> 54.5 us  [on_device(): lax.all_gather(lax.dynamic_slice_in_dim(obs_pert[0], half, share, 1), 'ti...]
    all_to_all x2 -> x1, waiting for transfers between devices: 56.9 us -> 6.08 us  [on_device(): lax.all_to_all(by_parity, ('tile', 'lev'), split_axis=0, concat_axis=0, t...]
    pallas_call x0 -> x2, Pallas kernels: none -> 36.5 us  [the longest x1 29 us: tile_dots(): pl.pallas_call(functools.partial(dots_kernel, bins), grid_spec=pltpu.Pref...]
    slice x1 -> x2, local copies, waits for them, and re-layouts: 8.46 us -> 43.6 us  [the longest x1 43.6 us: on_device(): weight_mine[0][None, :]]
    psum x1 -> x0, blocking collectives: 17.6 us -> none  [on_device(): summary = lax.psum(partial_value, 'lev').astype(jnp.bfloat16)]
    select_n x6 -> x1, other arithmetic: 14.3 us -> 0.56 us  [on_device(): jnp.where(last > first, (last + CHUNK - 1) // CHUNK, first_chunk)]
    dot_general x1 -> x0, matrix products: 10.9 us -> none  [on_device(): jnp.einsum('bl,klc->bck', local_vert, weighted, precision=lax.Precision.H...]
  transfers between devices with their start and end apart: 2 -> 4, of which waited for: 1 -> 3; matrix products, arithmetic and copies ran while one was open for 15% -> 33% of each run, Pallas kernels for 0% -> 4%
where the time goes in v1:
time: 192 us; the launch traced here: 190 us
  waiting for transfers between devices  65 us (34%)
  local copies, waits for them, and re-layouts  60.7 us (32%)
  Pallas kernels  36.5 us (19%)
  between operations  14.2 us (7%)
  other arithmetic  9.43 us (5%)
  starting transfers between devices  4.05 us (2%)
    all_gather x1, waiting for transfers between devices, on_device(): lax.all_gather(lax.dynamic_slice_in_dim(obs_pert[0], half, share, 1), 'ti...  54.5 us
    slice x1, local copies, waits for them, and re-layouts, on_device(): weight_mine[0][None, :]  43.6 us
    pallas_call x1, Pallas kernels, tile_dots(): pl.pallas_call(functools.partial(dots_kernel, bins), grid_spec=pltpu.Pref...  29 us
    pallas_call x1, Pallas kernels, partial_summary(): pl.pallas_call(functools.partial(partial_kernel, group), grid=(columns //...  7.47 us
    all_to_all x1, waiting for transfers between devices, on_device(): lax.all_to_all(by_parity, ('tile', 'lev'), split_axis=0, concat_axis=0, t...  6.08 us
    another operation x3, local copies, waits for them, and re-layouts, pick_level(): values.reshape(values.shape[:-1] + (values.shape[-1] // lev_count, lev_co...  6.02 us
    unnamed x3, waiting for transfers between devices  4.45 us
    unnamed x22, local copies, waits for them, and re-layouts  3.87 us
  transfers between devices with their start and end apart: 4, of which 3 were waited for; matrix products, arithmetic and copies ran while one was open for 33% of the time, Pallas kernels for 4%

profile of v1, /device:TPU:0, one launch (start us, length us, event | category | flops | bytes accessed | tf_op | source)
XLA Modules:
  0.0 189.9 jit_solution(4743586246352191776)
XLA Ops:
  6.5 0.0 copy-start
  6.5 0.0 all-reduce.3.cloned.1.call-start
  6.5 1.0 fusion.1
  7.5 0.8 fusion.3
  8.3 1.2 dynamic-slice.2
  10.2 0.7 dynamic-slice_add_fusion
  10.9 0.1 select_reduce_fusion.3
  11.0 0.1 concatenate.6
  11.1 0.3 dynamic-update-slice
  11.4 0.0 copy-start.2
  11.4 0.6 copy-done.2
  12.0 0.0 all-reduce.3.cloned.1.call-update
  12.1 0.0 all-gather.3.cloned.1.call-start
  12.1 0.0 copy-done
  12.1 0.8 constant_dynamic-slice_fusion
  12.9 0.0 all-gather.3.cloned.1.call-update
  12.9 0.8 constant_dynamic-slice_fusion.1
  13.7 0.2 broadcast_multiply_fusion
  13.8 0.4 mul.101
  14.3 0.6 pad_maximum_fusion.weight_ref
  14.9 0.0 copy-start.4
  14.9 0.0 copy-start.3
  14.9 7.5 %partial_summary.1 = (f32[8,80,2048]{2,1,0:T(8,128)}, bf16[8,80,2048]{2,1,0:T(8,128)(2,1)}) custom-call(bf16[80,16,2048]{2,1,0:T(8,128)(2,1)} %members_ref.1, bf16[16,2048]{1,0:T(8,128)(2,1)} %early_ref.1, bf16[16,2048]{1,0:T(8,128)(2,1)} %late_ref.1, bf16[16,2048]{1,0:T(8,128)(2,1)} %energy_ref.1, bf16[256,256]{1,0:T(8,128)(2,1)} %pad_maximum_fusion.weight_ref), custom_call_target="tpu_custom_call" | custom-call | tf_op jit(solution)/shard_map/partial_summary/pallas_call | solution.py:55
  22.4 0.0 copy-start.5
  22.4 0.0 copy-start.6
  22.4 0.5 collective-permute-start
  22.9 0.5 broadcast.83
  23.5 0.0 copy-done.4
  23.5 0.7 reduce.34
  24.1 2.0 %reshape_squeeze.15 = s32[2048,2]{1,0:T(8,128)} reshape(s32[4096]{0:T(1024)S(1)} %reduce.34) | data formatting | bytes 32768 | tf_op jit(solution)/shard_map/reshape;squeeze | solution.py:16
  26.2 0.0 copy-done.3
  26.2 0.6 copy.21
  26.8 0.0 copy-start.7
  26.8 0.5 broadcast.81
  27.3 0.0 copy-done.5
  27.3 0.7 reduce.33
  28.0 2.0 %reshape_squeeze.12 = f32[2048,2]{1,0:T(8,128)} reshape(f32[4096]{0:T(1024)S(1)} %reduce.33) | data formatting | bytes 32768 | tf_op jit(solution)/shard_map/reshape;squeeze | solution.py:16
  30.0 0.0 copy-done.6
  30.0 0.7 reduce.32
  30.7 2.0 %reshape_squeeze.13 = f32[2048,2]{1,0:T(8,128)} reshape(f32[4096]{0:T(1024)S(1)} %reduce.32) | data formatting | bytes 32768 | tf_op jit(solution)/shard_map/reshape;squeeze | solution.py:16
  32.7 2.4 %multiply_reduce_fusion = f32[2048]{0:T(1024)S(1)} fusion(f32[2048,2]{1,0:T(8,128)} %reshape_squeeze.13, s32[]{:T(128)S(6)} %select_n.58, f32[2048,2]{1,0:T(8,128)} %reshape_squeeze.12), kind=kLoop, calls=%fused_computation.5 | loop fusion | flops 4096 | bytes 24580 | tf_op jit(solution)/shard_map/div | solution.py:216
  35.2 0.0 copy-done.7
  35.2 0.2 slice_reduce_fusion.2
  35.4 43.6 %dynamic-slice_reduce_fusion.3 = (f32[2048]{0:T(1024)S(1)}, f32[2048]{0:T(1024)S(1)}, f32[2048]{0:T(1024)S(1)}, f32[2048]{0:T(1024)S(1)}) fusion(f32[4,2048,2]{0,2,1:T(2,128)S(1)} %bitcast.12, s32[]{:T(128)S(6)} %select_n.58, s32[]{:T(128)S(6)} %add.76, s32[]{:T(128)S(6)} %add.75, s32[]{:T(128)S(6)} %add.77), kind=kLoop, calls=%fused_computation.3 | loop fusion | bytes 65552 | tf_op jit(solution)/shard_map/slice | solution.py:209
  79.0 4.4 %all-reduce.3.cloned.1.call-done = s32[16512]{0:T(1024)} async-done(((s32[16512]{0:T(1024)}), s32[16512]{0:T(1024)}) %all-reduce.3.cloned.1.call-update) | async-done | bytes 66064
  83.4 1.0 reshape.88
  84.4 0.7 reshape.85.lookup_ref
  85.1 0.2 dynamic-slice_reduce_fusion.5
  85.3 0.6 compare_select_fusion
  85.8 0.0 collective-permute-done.other_ref
  85.8 54.5 %all-gather.3.cloned.1.call-done.pert_ref = bf16[8,80,2048]{2,1,0:T(8,128)(2,1)} async-done(((bf16[1,80,2048]{2,1,0:T(8,128)(2,1)}), bf16[8,80,2048]{2,1,0:T(8,128)(2,1)}) %all-gather.3.cloned.1.call-update) | async-done | bytes 2621456 | tf_op jit(solution)/shard_map/all_gather | solution.py:174
  140.3 29.0 %tile_dots.1 = f32[8,1,2048]{2,1,0:T(1,128)} custom-call(s32[8]{0:T(128)} %get-tuple-element.28.first_ref, s32[8]{0:T(128)} %get-tuple-element.27.last_ref, f32[8,80,2048]{2,1,0:T(8,128)} %get-tuple-element.7.own_ref, bf16[8,80,2048]{2,1,0:T(8,128)(2,1)} %collective-permute-done.other_ref, s32[8,1,2048]{2,1,0:T(1,128)} %reshape.85.lookup_ref, ...), custom_call_target="tpu_custom_call" | custom-call | tf_op jit(solution)/shard_map/tile_dots/pallas_call | solution.py:120
  169.3 0.0 copy-start.1
  169.3 1.3 copy.22
  170.6 0.4 copy.23
  171.1 0.7 all_to_all.8
  171.8 3.5 %all-to-all-start = ((f32[16,1,1024]{2,1,0:T(1,128)}), f32[16,1,1024]{2,1,0:T(1,128)S(1)}, u32[]{:S(2)}, u32[]{:S(2)}) async-start(f32[16,1,1024]{2,1,0:T(1,128)} %all_to_all.8), calls=%async_computation | async-start | bytes 131072 | tf_op jit(solution)/shard_map/all_to_all | solution.py:203
  175.3 0.0 copy-done.1
  175.3 0.6 dynamic-slice_reduce_fusion.4
  175.9 0.1 select_reduce_fusion.2
  176.1 6.1 %all-to-all-done = f32[16,1,1024]{2,1,0:T(1,128)S(1)} async-done(((f32[16,1,1024]{2,1,0:T(1,128)}), f32[16,1,1024]{2,1,0:T(1,128)S(1)}, u32[]{:S(2)}, u32[]{:S(2)}) %all-to-all-start) | async-done | bytes 65568 | tf_op jit(solution)/shard_map/all_to_all | solution.py:203
  182.2 0.2 reduce.14
  182.3 0.1 multiply_reduce_fusion.1
  182.4 0.6 mul.103
  (7 shorter events, 0.1 us)
Async XLA Ops:
  6.5 5.6 %copy-start = (bf16[1,80,4096]{2,1,0:T(8,128)(2,1)S(1)}, bf16[1,80,4096]{2,1,0:T(8,128)(2,1)}, u32[]{:S(2)}) copy-start(bf16[1,80,4096]{2,1,0:T(8,128)(2,1)} %param.22) | copy-start | bytes 1966084
  6.5 76.9 %all-reduce.3.cloned.1.call-start = ((), (), s32[]{:S(2)}) async-start(), calls=%async_computation.2 | async-start | bytes 139264
  11.4 0.6 copy-start.2
  12.1 128.2 %all-gather.3.cloned.1.call-start = ((), (), s32[]{:S(2)}) async-start(), calls=%async_computation.1 | async-start | bytes 2949120 | tf_op jit(solution)/shard_map/all_gather | solution.py:174
  14.9 8.5 %copy-start.4 = (s32[1,4096]{1,0:T(1,128)S(1)}, s32[1,4096]{1,0:T(1,128)}, u32[]{:S(2)}) copy-start(s32[1,4096]{1,0:T(1,128)} %param.19) | copy-start | bytes 49156
  14.9 11.2 %copy-start.3 = (f32[1,4,4096]{2,1,0:T(4,128)S(1)}, f32[1,4,4096]{2,1,0:T(4,128)}, u32[]{:S(2)}) copy-start(f32[1,4,4096]{2,1,0:T(4,128)} %param.25) | copy-start | bytes 196612
  22.4 4.9 %copy-start.5 = (f32[1,4096]{1,0:T(1,128)S(1)}, f32[1,4096]{1,0:T(1,128)}, u32[]{:S(2)}) copy-start(f32[1,4096]{1,0:T(1,128)} %param.23) | copy-start | bytes 49156
  22.4 7.6 %copy-start.6 = (f32[1,4096]{1,0:T(1,128)S(1)}, f32[1,4096]{1,0:T(1,128)}, u32[]{:S(2)}) copy-start(f32[1,4096]{1,0:T(1,128)} %param.24) | copy-start | bytes 49156
  22.4 63.4 %collective-permute-start = (bf16[8,80,2048]{2,1,0:T(8,128)(2,1)}, bf16[8,80,2048]{2,1,0:T(8,128)(2,1)}, u32[]{:S(2)}, u32[]{:S(2)}) collective-permute-start(bf16[8,80,2048]{2,1,0:T(8,128)(2,1)} %get-tuple-element.8), channel_id=1, source_target_pairs={{0,1},{1,0},{2,3},{3,2},{4,5},{5,4},{6,7},{7,6},{8,9},{9,8},{10,11... | collective-permute-start | bytes 7864328 | tf_op jit(solution)/shard_map/ppermute | solution.py:198
  26.8 8.4 %copy-start.7 = (s32[1,2,3]{2,1,0:T(2,128)S(1)}, s32[1,2,3]{2,1,0:T(2,128)}, u32[]{:S(2)}) copy-start(s32[1,2,3]{2,1,0:T(2,128)} %param.18) | copy-start | bytes 76
  169.3 6.0 %copy-start.1 = (s32[2048,2]{1,0:T(8,128)S(1)}, s32[2048,2]{1,0:T(8,128)}, u32[]{:S(2)}) copy-start(s32[2048,2]{1,0:T(8,128)} %reshape_squeeze.15) | copy-start | bytes 49156
  171.8 10.4 %all-to-all-start = ((f32[16,1,1024]{2,1,0:T(1,128)}), f32[16,1,1024]{2,1,0:T(1,128)S(1)}, u32[]{:S(2)}, u32[]{:S(2)}) async-start(f32[16,1,1024]{2,1,0:T(1,128)} %all_to_all.8), calls=%async_computation | async-start | bytes 131072 | tf_op jit(solution)/shard_map/all_to_all | solution.py:203
Sparse Core Ops, SparseCore 0:
  12.2 71.1 all-reduce.2
  85.6 54.6 all-gather.2
